TPU v7x, 128 devices: a whole 4x4x4 slice. The times are simulated.
128 devices in a mesh: dp: 16 (over y, z_lo, core), tensor: 8 (over x, z_hi).
Axes of the slice: x: 4, y: 4, z: 4 (z_hi: 2, z_lo: 2; z = z_hi * 2 + z_lo), core: 2. Of those that a mesh axis runs over, the one named last changes fastest.
Arguments:
- llm_grad: bfloat16 [16384, 3072], P('tensor', 'dp'), may hold values from -6 to 6
- image_slot: int32 [64], replicated, may hold values from 0 to 63, each once
- pre_act: bfloat16 [16384, 12288], P('dp', 'tensor'), may hold values from -8 to 8
- w_down: bfloat16 [12288, 3072], P('tensor'), may hold values from -0.0546875 to 0.0546875
Outputs:
- grad_pre: bfloat16 [16384, 12288], P('dp', 'tensor')
- grad_down: float32 [12288, 3072], P('tensor', 'dp')
Inputs may be any that keep to these rules, and one draw needn't show every extreme that they name: `image_slot`: each image slot is named by exactly one encoder image.
All inputs are finite; a program needn't handle non-finite values.
Results may differ from a plain program's by a relative error of at most 0.0027.
Values may be sent and summed in bfloat16 or wider, within the bound.
A program may use at most 128 MiB of HBM per device.

v0:
```python
import jax
import jax.numpy as jnp
from jax import lax
from jax.sharding import PartitionSpec as P

PATCH = 256


def gelu_parts(value):
    inner = 0.7978845608 * (value + 0.044715 * value * value * value)
    tanh_value = jnp.tanh(inner)
    out = 0.5 * value * (1.0 + tanh_value)
    slope = 0.5 * (1.0 + tanh_value) + 0.5 * value * (
        1.0 - tanh_value * tanh_value
    ) * 0.7978845608 * (1.0 + 3.0 * 0.044715 * value * value)
    return (out, slope)


def on_device(llm_grad, image_slot, pre_act, w_down):
    tok_rows = pre_act.shape[0]
    data_count = lax.axis_size("dp")
    feat_cols = llm_grad.shape[1]
    slots = lax.all_gather(llm_grad, "tensor", axis=0, tiled=True)
    blocks = slots.reshape(slots.shape[0] // PATCH, PATCH, feat_cols)
    picked = blocks[image_slot].reshape(data_count, tok_rows, feat_cols)
    out_grad = lax.all_to_all(
        picked.reshape(data_count * tok_rows, feat_cols),
        "dp",
        split_axis=0,
        concat_axis=1,
        tiled=True,
    )
    hidden_f, slope = gelu_parts(pre_act.astype(jnp.float32))
    hidden = hidden_f.astype(jnp.bfloat16)
    grad_hidden = lax.dot_general(
        out_grad, w_down, (((1,), (1,)), ((), ())), preferred_element_type=jnp.float32
    )
    grad_pre = (grad_hidden * slope).astype(jnp.bfloat16)
    scale_factor = 1.0 / jnp.sqrt(jnp.float32(tok_rows * data_count))
    product = lax.dot_general(
        out_grad, hidden, (((0,), (0,)), ((), ())), preferred_element_type=jnp.float32
    )
    summed = lax.psum_scatter(product * scale_factor, "dp", scatter_dimension=0, tiled=True)
    return (grad_pre, summed.T)


def solution(mesh):
    placed = (P("tensor", "dp"), P(), P("dp", "tensor"), P("tensor", None))
    return jax.shard_map(
        on_device,
        mesh=mesh,
        in_specs=placed,
        out_specs=(P("dp", "tensor"), P("tensor", "dp")),
        check_vma=False,
    )
```

profile of v0, /device:TPU:1, one launch (start us, length us, event | category | flops | bytes accessed | tf_op | source)
XLA Modules:
  0.0 441.2 jit_solution(16743876930334034551)
XLA Ops:
  7.2 0.0 all-gather.2.cloned.1.call-start
  7.2 0.7 all-gather.2.cloned.1.call-update
  7.9 0.0 reduce-scatter.2.cloned.1.call-start
  7.9 0.7 compare_select_fusion
  8.6 94.2 %all-gather.2.cloned.1.call-done = bf16[16384,192]{0,1:T(8,128)(2,1)} async-done(((bf16[2048,192]{0,1:T(8,128)(2,1)}), bf16[16384,192]{0,1:T(8,128)(2,1)}) %all-gather.2.cloned.1.call-update) | async-done | bytes 6291472 | tf_op jit(solution)/shard_map/all_gather | solution.py:23
  102.8 6.3 %copy.14 = bf16[24,64,8,256]{3,2,0,1:T(8,128)(2,1)} copy(bf16[24,64,8,256]{3,2,1,0:T(8,128)(2,1)} %bitcast.14) | data formatting | bytes 12582912 | tf_op jit(solution)/shard_map/reshape | solution.py:24
  109.1 6.4 %gather_fusion = bf16[64,256,192]{1,2,0:T(8,128)(2,1)} fusion(bf16[64,256,192]{1,2,0:T(8,128)(2,1)} %bitcast.13, s32[1024]{0:T(1024)S(1)} %pad_clamp_fusion), kind=kCustom, calls=%fused_computation | custom fusion | bytes 12583168 | tf_op jit(solution)/shard_map/gather | solution.py:25
  115.5 9.0 %copy.10 = bf16[64,256,192]{1,0,2:T(8,128)(2,1)} copy(bf16[64,256,192]{1,2,0:T(8,128)(2,1)} %gather_fusion) | data formatting | bytes 12582912 | tf_op jit(solution)/shard_map/gather | solution.py:25
  124.5 10.7 %all_to_all.14 = bf16[16,1024,192]{1,0,2:T(8,128)(2,1)} reshape(bf16[64,256,192]{1,0,2:T(8,128)(2,1)} %copy.10) | data formatting | bytes 12582912 | tf_op jit(solution)/shard_map/all_to_all | solution.py:26
  135.2 6.3 %copy.11 = bf16[16,1024,192]{1,2,0:T(8,128)(2,1)S(1)} copy(bf16[16,1024,192]{1,0,2:T(8,128)(2,1)} %all_to_all.14) | data formatting | bytes 12582912 | tf_op jit(solution)/shard_map/all_to_all | solution.py:26
  141.5 0.0 copy-start.1
  141.5 77.0 %all_to_all.19 = bf16[16,1024,192]{1,2,0:T(8,128)(2,1)S(1)} all-to-all(bf16[16,1024,192]{1,2,0:T(8,128)(2,1)S(1)} %copy.11), channel_id=1, replica_groups=mesh['dp'=16,'tensor'=8] {'dp'}, dimensions={0} | all-to-all | bytes 12582912 | tf_op jit(solution)/shard_map/all_to_all | solution.py:26
  218.5 0.0 copy-start
  218.5 2.6 copy-done
  221.1 0.0 copy-done.1
  221.1 14.0 %convolution_multiply_fusion = f32[3072,1536]{1,0:T(8,128)} fusion(bf16[1024,3072]{0,1:T(8,128)(2,1)S(1)} %bitcast.15, bf16[1024,1536]{1,0:T(8,128)(2,1)S(1)} %copy-done.1), kind=kOutput, calls=%fused_computation.8 | convolution fusion | flops 9684123648 | bytes 28311552 | tf_op jit(solution)/shard_map/dot_general | solution.py:40
  235.0 0.0 reduce-scatter.2.cloned.1.call-update
  235.0 18.8 %fusion.6 = bf16[1024,1536]{1,0:T(8,128)(2,1)} fusion(bf16[1024,1536]{1,0:T(8,128)(2,1)S(1)} %copy-done.1, bf16[1024,3072]{0,1:T(8,128)(2,1)} %bitcast.16, bf16[1536,3072]{1,0:T(8,128)(2,1)} %param.7), kind=kOutput, calls=%fused_computation.15 | convolution fusion | flops 9695133696 | bytes 22020096 | tf_op jit(solution)/shard_map/dot_general | solution.py:35
  253.9 180.5 %reduce-scatter.2.cloned.1.call-done = f32[192,1536]{1,0:T(8,128)} async-done(((f32[3072,1536]{1,0:T(8,128)}), f32[192,1536]{1,0:T(8,128)}) %reduce-scatter.2.cloned.1.call-update) | async-done | bytes 1179664 | tf_op jit(solution)/shard_map/reduce_scatter | solution.py:43
  (1 shorter events, 0.0 us)
Async XLA Ops:
  7.2 95.7 %all-gather.2.cloned.1.call-start = ((), (), s32[]{:S(2)}) async-start(), calls=%async_computation.2 | async-start | bytes 7077888 | tf_op jit(solution)/shard_map/all_gather | solution.py:23
  7.9 426.5 %reduce-scatter.2.cloned.1.call-start = ((), (), s32[]{:S(2)}) async-start(), calls=%async_computation.3 | async-start | bytes 20054016 | tf_op jit(solution)/shard_map/reduce_scatter | solution.py:43
  141.5 79.6 %copy-start.1 = (bf16[1024,1536]{1,0:T(8,128)(2,1)S(1)}, bf16[1024,1536]{1,0:T(8,128)(2,1)}, u32[]{:S(2)}) copy-start(bf16[1024,1536]{1,0:T(8,128)(2,1)} %param.6) | copy-start | bytes 9437188
  218.5 2.6 copy-start
Sparse Core Ops, SparseCore 0:
  10.4 92.4 all-gather.1
  235.2 199.1 reduce-scatter.1
where the time goes:
time: 442 us; the launch traced here: 441 us
  waiting for transfers between devices  275 us (62%)
  blocking collectives  77 us (17%)
  local copies, waits for them, and re-layouts  41.3 us (9%)
  matrix products  32.8 us (7%)
  between operations  14.1 us (3%)
    reduce_scatter x1, waiting for transfers between devices, on_device(): lax.psum_scatter(product * scale_factor, 'dp', scatter_dimension=0, tiled...  180 us
    all_gather x1, waiting for transfers between devices, on_device(): slots = lax.all_gather(llm_grad, 'tensor', axis=0, tiled=True)  94.2 us
    all_to_all x1, blocking collectives, on_device(): lax.all_to_all(picked.reshape(data_count * tok_rows, feat_cols), 'dp', sp...  77 us
    dot_general x1, matrix products, on_device(): lax.dot_general(out_grad, w_down, (((1,), (1,)), ((), ())), preferred_ele...  18.8 us
    all_to_all x2, local copies, waits for them, and re-layouts, on_device(): lax.all_to_all(picked.reshape(data_count * tok_rows, feat_cols), 'dp', sp...  17 us
    gather x2, local copies, waits for them, and re-layouts, on_device(): picked = blocks[image_slot].reshape(data_count, tok_rows, feat_cols)  15.4 us
    dot_general x1, matrix products, on_device(): lax.dot_general(out_grad, hidden, (((0,), (0,)), ((), ())), preferred_ele...  14 us
  transfers between devices with their start and end apart: 2, of which 2 were waited for; matrix products, arithmetic and copies ran while one was open for 4% of the time, Pallas kernels for 0%

commit v1 on v0

v1 whole, which is shorter than its diff:
```python
import jax
import jax.numpy as jnp
from jax import lax
from jax.experimental import pallas as pl
from jax.experimental.pallas import tpu as pltpu
from jax.sharding import PartitionSpec as P

MESH = pl.DeviceIdType.MESH
BF = jnp.bfloat16
F32 = jnp.float32
NK = 3
TOK = 1024
NF = 1536


def gelu_parts(value):
    inner = 0.7978845608 * (value + 0.044715 * value * value * value)
    tanh_value = jnp.tanh(inner)
    out = 0.5 * value * (1.0 + tanh_value)
    slope = 0.5 * (1.0 + tanh_value) + 0.5 * value * (
        1.0 - tanh_value * tanh_value
    ) * 0.7978845608 * (1.0 + 3.0 * 0.044715 * value * value)
    return (out, slope)


def kernel(
    slot_ref, llm_hbm, pre_hbm, w_hbm, gp_hbm, gd_hbm,
    llm, pre, w, send_t, recv_t0, recv_t1, recv_t2, send_d, own, sib, hid,
    left, acc, send_r, recv_r, mine, send_z, recv_z, fin, rhs, gp,
    in_sem, out_sem, t_ss, t_rs, d_ss, d_rs, g_ss, g_rs, s_ss, s_rs, h_ss, h_rs,
    r_ss, r_rs, z_ss, z_rs,
):
    recv_t = (recv_t0, recv_t1, recv_t2)
    dp = lax.axis_index("dp")
    j = lax.axis_index("tensor")
    y, zlo, c = dp // 4, (dp // 2) % 2, dp % 2
    x, zhi = j // 2, j % 2
    q = dp // 2

    def dev_t(o):
        return (dp, (j + o) % 8)

    def dev_q(o):
        return (((q + o) % 8) * 2 + c, j)

    sibling = (dp - c + (1 - c), j)
    z2 = (dp, 2 * x + (1 - zhi))
    xr, xl, xo = (x + 1) % 4, (x + 3) % 4, (x + 2) % 4
    dev_xr, dev_xl = (dp, 2 * xr + zhi), (dp, 2 * xl + zhi)
    zpart = ((y * 2 + (1 - zlo)) * 2 + c, j)

    def dev_y(o):
        return ((((y + o) % 4) * 2 + zlo) * 2 + c, j)

    def rcopy(src, dst, ss, rs, dev):
        return pltpu.make_async_remote_copy(
            src_ref=src, dst_ref=dst, send_sem=ss, recv_sem=rs, device_id=dev, device_id_type=MESH
        )

    sends = []

    def send(src, dst, ss, rs, dev):
        cp = rcopy(src, dst, ss, rs, dev)
        cp.start()
        sends.append(cp)

    def await_recv(land, ss, rs, dev):
        rcopy(land, land, ss, rs, dev).wait_recv()

    cp_llm = pltpu.make_async_copy(llm_hbm, llm, in_sem.at[0])
    cp_pre = pltpu.make_async_copy(pre_hbm, pre, in_sem.at[1])
    cp_w = pltpu.make_async_copy(w_hbm, w, in_sem.at[2])
    cp_llm.start()
    cp_pre.start()
    cp_w.start()
    barrier = pltpu.get_barrier_semaphore()
    for o in range(1, 8):
        pl.semaphore_signal(barrier, inc=1, device_id=dev_t(o), device_id_type=MESH)
        pl.semaphore_signal(barrier, inc=1, device_id=dev_q(o), device_id_type=MESH)
    pl.semaphore_signal(barrier, inc=1, device_id=sibling, device_id_type=MESH)
    cp_llm.wait()

    @pl.loop(0, 8)
    def _(s):
        for h in range(2):
            rows = pl.ds(pl.multiple_of(s * 256 + h * 128, 128), 128)
            flipped = llm[rows, :].T
            for cq in range(4):
                for k in range(NK):
                    send_t[k, cq * 2 + h, s] = flipped[48 * cq + 16 * k : 48 * cq + 16 * k + 16, :]

    pl.semaphore_wait(barrier, 15)

    def t_send(k):
        for o in range(1, 8):
            send(
                send_t.at[k, (j + o) % 8], recv_t[k].at[pl.ds(j * 8, 8)],
                t_ss.at[k, o], t_rs.at[k, o], dev_t(o),
            )
        recv_t[k][pl.ds(j * 8, 8)] = send_t[k, j]

    def t_wait_d_send(k):
        for o in range(1, 8):
            await_recv(recv_t[k].at[pl.ds(((j + 8 - o) % 8) * 8, 8)], t_ss.at[k, o], t_rs.at[k, o], dev_t(o))

        @pl.loop(0, 64)
        def _(e):
            send_d[k, e // 8, e % 8] = recv_t[k][slot_ref[e]]

        for o in range(1, 8):
            send(
                send_d.at[k, (q + o) % 8], own.at[k, j, q], d_ss.at[k, o], d_rs.at[k, o], dev_q(o)
            )
        own[k, j, q] = send_d[k, q]

    def d_wait(k):
        for o in range(1, 8):
            await_recv(own.at[k, j, (q + 8 - o) % 8], d_ss.at[k, o], d_rs.at[k, o], dev_q(o))

    def piece(k, xx, zz):
        return own.at[k, 2 * xx + zz]

    LO, HI = pl.ds(0, 4), pl.ds(4, 4)

    def half(k, xx, zz, part):
        return own.at[k, 2 * xx + zz, part]

    def g_send(k, n, ref, dev):
        send(ref, ref, g_ss.at[k, n], g_rs.at[k, n], dev)

    def g_wait(k, n, ref, dev):
        await_recv(ref, g_ss.at[k, n], g_rs.at[k, n], dev)

    oz = 1 - zhi

    def g_z(k):
        g_send(k, 0, piece(k, x, zhi), z2)

    def g_x(k):
        g_send(k, 1, piece(k, x, zhi), dev_xr)
        g_send(k, 2, piece(k, x, zhi), dev_xl)

    def g_b(k):
        g_wait(k, 0, piece(k, x, oz), z2)
        g_send(k, 3, piece(k, x, oz), dev_xr)
        g_send(k, 4, piece(k, x, oz), dev_xl)

    def g_c(k):
        g_wait(k, 1, piece(k, xl, zhi), dev_xl)
        g_send(k, 5, half(k, xl, zhi, LO), dev_xr)
        g_wait(k, 2, piece(k, xr, zhi), dev_xr)
        g_send(k, 6, half(k, xr, zhi, HI), dev_xl)

    def g_e(k):
        g_wait(k, 3, piece(k, xl, oz), dev_xl)
        g_send(k, 7, half(k, xl, oz, LO), dev_xr)
        g_wait(k, 4, piece(k, xr, oz), dev_xr)
        g_send(k, 8, half(k, xr, oz, HI), dev_xl)

    def g_f(k):
        g_wait(k, 5, half(k, xo, zhi, LO), dev_xl)
        g_wait(k, 6, half(k, xo, zhi, HI), dev_xr)
        g_wait(k, 7, half(k, xo, oz, LO), dev_xl)
        g_wait(k, 8, half(k, xo, oz, HI), dev_xr)
        send(
            own.at[k, :, :, pl.ds((1 - c) * 4, 4)], sib.at[k], s_ss.at[k], s_rs.at[k], sibling
        )

    def hidden_rows(first, count):
        @pl.loop(first, first + count)
        def _(b):
            rows = pl.ds(pl.multiple_of(b * 32, 32), 32)
            value, _ = gelu_parts(pre[rows, :].astype(F32))
            hid[pl.ds(pl.multiple_of(c * TOK + b * 32, 32), 32), :] = value.astype(BF)

    def down(k):
        @pl.loop(0, 8)
        def _(qq):
            for cq in range(4):
                row = pl.ds(pl.multiple_of(qq * 64 + cq * 16, 16), 16)
                for img in range(8):
                    for h in range(2):
                        left[row, (img * 2 + h) * 128 : (img * 2 + h + 1) * 128] = own[
                            k, cq * 2 + h, qq, img
                        ]

        @pl.loop(0, 6)
        def _(n):
            cols = pl.ds(pl.multiple_of(n * 256, 256), 256)
            part = jnp.dot(left[...], hid[:, cols], preferred_element_type=F32)
            part = part.reshape(8, 64, 256)
            acc[:, :, cols] = part
            send_r[k, :, :, cols] = part.astype(BF)

        for o in (2, 1, 3):
            send(
                send_r.at[k, pl.ds(((y + o) % 4) * 2, 2)], recv_r.at[k, o - 1],
                r_ss.at[k, o], r_rs.at[k, o], dev_y(o),
            )
        mine[k] = acc[pl.ds(y * 2, 2)]

    def r_sum(k):
        for o in (1, 2, 3):
            await_recv(recv_r.at[k, o - 1], r_ss.at[k, o], r_rs.at[k, o], dev_y(o))

        @pl.loop(0, 4)
        def _(b):
            rows = pl.ds(pl.multiple_of(b * 16, 16), 16)
            for side in range(2):
                zz = zlo if side == 0 else 1 - zlo
                total = mine[k, zz, rows, :]
                for o in range(3):
                    total += recv_r[k, o, zz, rows, :].astype(F32)
                if side == 0:
                    mine[k, zz, rows, :] = total
                else:
                    send_z[k, rows, :] = total.astype(BF)

        send(send_z.at[k], recv_z.at[k], z_ss.at[k], z_rs.at[k], zpart)

    def r_final(k):
        await_recv(recv_z.at[k], z_ss.at[k], z_rs.at[k], zpart)

        @pl.loop(0, 4)
        def _(cq):
            rows = pl.ds(pl.multiple_of(cq * 16, 16), 16)
            total = mine[k, zlo, rows, :] + recv_z[k, rows, :].astype(F32)
            fin[pl.ds(pl.multiple_of(cq * 48 + k * 16, 16), 16), :] = total * (1.0 / 128.0)

    def up(b):
        @pl.loop(0, 8)
        def _(qq):
            for cq in range(4):
                for k in range(NK):
                    for h in range(2):
                        lanes = slice(h * 128, (h + 1) * 128)
                        at = qq * 384 + cq * 48 + k * 16
                        rhs[pl.ds(pl.multiple_of(at + c * 192, 16), 16), lanes] = own[
                            k, cq * 2 + h, qq, c * 4 + b
                        ]
                        rhs[pl.ds(pl.multiple_of(at + (1 - c) * 192, 16), 16), lanes] = sib[
                            k, cq * 2 + h, qq, b
                        ]

        @pl.loop(0, 3)
        def _(n):
            fs = pl.ds(pl.multiple_of(n * 512, 512), 512)
            part = jnp.dot(w[fs, :], rhs[...], preferred_element_type=F32)
            _, slope = gelu_parts(pre[b * 256 : (b + 1) * 256, fs].astype(F32))
            gp[b * 256 : (b + 1) * 256, fs] = (part.T * slope).astype(BF)

        rows = pl.ds(b * 256, 256)
        cp = pltpu.make_async_copy(gp.at[rows], gp_hbm.at[rows], out_sem.at[b])
        cp.start()
        return cp

    t_send(0)
    t_send(1)
    t_send(2)
    cp_pre.wait()
    hidden_rows(0, 8)
    t_wait_d_send(0)
    t_wait_d_send(1)
    hidden_rows(8, 4)
    d_wait(0)
    g_z(0)
    g_x(0)
    t_wait_d_send(2)
    hidden_rows(12, 8)
    g_b(0)
    hidden_rows(20, 6)
    d_wait(1)
    g_z(1)
    g_c(0)
    hidden_rows(26, 6)
    send(
        hid.at[pl.ds(c * TOK, TOK)], hid.at[pl.ds(c * TOK, TOK)], h_ss.at[0], h_rs.at[0], sibling
    )
    g_e(0)
    g_x(1)
    g_b(1)
    d_wait(2)
    g_z(2)
    g_f(0)
    await_recv(hid.at[pl.ds((1 - c) * TOK, TOK)], h_ss.at[0], h_rs.at[0], sibling)
    down(0)
    g_c(1)
    g_e(1)
    g_x(2)
    g_b(2)
    g_f(1)
    down(1)
    g_c(2)
    g_e(2)
    r_sum(0)
    g_f(2)
    down(2)
    r_final(0)
    cp_w.wait()
    for k in range(NK):
        await_recv(sib.at[k], s_ss.at[k], s_rs.at[k], sibling)
    outs = [up(0)]
    r_sum(1)
    outs.append(up(1))
    outs.append(up(2))
    r_final(1)
    outs.append(up(3))
    r_sum(2)
    r_final(2)
    cp = pltpu.make_async_copy(fin, gd_hbm, out_sem.at[4])
    cp.start()
    outs.append(cp)
    for cp in outs:
        cp.wait()
    for cp in sends:
        cp.wait_send()


def on_device(llm_grad, image_slot, pre_act, w_down):
    dma = pltpu.SemaphoreType.DMA
    any_space = pl.BlockSpec(memory_space=pl.ANY)
    grad_pre, down = pl.pallas_call(
        kernel,
        out_shape=(
            jax.ShapeDtypeStruct((TOK, NF), BF),
            jax.ShapeDtypeStruct((192, NF), F32),
        ),
        in_specs=[pl.BlockSpec(memory_space=pltpu.SMEM), any_space, any_space, any_space],
        out_specs=(any_space, any_space),
        scratch_shapes=[
            pltpu.VMEM((2048, 192), BF),
            pltpu.VMEM((TOK, NF), BF),
            pltpu.VMEM((NF, 3072), BF),
            pltpu.VMEM((NK, 8, 8, 16, 128), BF),
            pltpu.VMEM((64, 16, 128), BF),
            pltpu.VMEM((64, 16, 128), BF),
            pltpu.VMEM((64, 16, 128), BF),
            pltpu.VMEM((NK, 8, 8, 16, 128), BF),
            pltpu.VMEM((NK, 8, 8, 8, 16, 128), BF),
            pltpu.VMEM((NK, 8, 8, 4, 16, 128), BF),
            pltpu.VMEM((2 * TOK, NF), BF),
            pltpu.VMEM((512, 2048), BF),
            pltpu.VMEM((8, 64, NF), F32),
            pltpu.VMEM((NK, 8, 64, NF), BF),
            pltpu.VMEM((NK, 3, 2, 64, NF), BF),
            pltpu.VMEM((NK, 2, 64, NF), F32),
            pltpu.VMEM((NK, 64, NF), BF),
            pltpu.VMEM((NK, 64, NF), BF),
            pltpu.VMEM((192, NF), F32),
            pltpu.VMEM((3072, 256), BF),
            pltpu.VMEM((TOK, NF), BF),
            dma((3,)), dma((5,)),
            dma((NK, 8)), dma((NK, 8)), dma((NK, 8)), dma((NK, 8)),
            dma((NK, 9)), dma((NK, 9)), dma((NK,)), dma((NK,)), dma((1,)), dma((1,)),
            dma((NK, 4)), dma((NK, 4)), dma((NK,)), dma((NK,)),
        ],
        compiler_params=pltpu.CompilerParams(
            collective_id=0, has_side_effects=True, vmem_limit_bytes=60 << 20
        ),
        cost_estimate=pl.CostEstimate(
            flops=19_327_352_832, bytes_accessed=18 << 20, transcendentals=3_000_000
        ),
    )(image_slot, llm_grad, pre_act, w_down)
    return (grad_pre, down.T)


def solution(mesh):
    placed = (P("tensor", "dp"), P(), P("dp", "tensor"), P("tensor", None))
    return jax.shard_map(
        on_device,
        mesh=mesh,
        in_specs=placed,
        out_specs=(P("dp", "tensor"), P("tensor", "dp")),
        check_vma=False,
    )
```

time: 442 us -> 118 us (0.27)
  waiting for transfers between devices: 275 us -> 0 us
  Pallas kernels: 0 us -> 110 us
  blocking collectives: 77 us -> 0 us
  local copies, waits for them, and re-layouts: 41.3 us -> 7.09 us
  matrix products: 32.8 us -> 0 us
  between operations: 14.1 us -> 0.65 us
    reduce_scatter x1 -> x0, waiting for transfers between devices: 180 us -> none  [on_device(): lax.psum_scatter(product * scale_factor, 'dp', scatter_dimension=0, tiled...]
    pallas_call x0 -> x1, Pallas kernels: none -> 110 us  [on_device(): pl.pallas_call(kernel, out_shape=(jax.ShapeDtypeStruct((TOK, NF), BF), ja...]
    all_gather x1 -> x0, waiting for transfers between devices: 94.2 us -> none  [on_device(): slots = lax.all_gather(llm_grad, 'tensor', axis=0, tiled=True)]
    all_to_all x1 -> x0, blocking collectives: 77 us -> none  [on_device(): lax.all_to_all(picked.reshape(data_count * tok_rows, feat_cols), 'dp', sp...]
    dot_general x2 -> x0, matrix products: 32.8 us -> none  [the longest x1 18.8 us: on_device(): lax.dot_general(out_grad, w_down, (((1,), (1,)), ((), ())), preferred_ele...]
    all_to_all x2 -> x0, local copies, waits for them, and re-layouts: 17 us -> none  [on_device(): lax.all_to_all(picked.reshape(data_count * tok_rows, feat_cols), 'dp', sp...]
    gather x2 -> x0, local copies, waits for them, and re-layouts: 15.4 us -> none  [on_device(): picked = blocks[image_slot].reshape(data_count, tok_rows, feat_cols)]
    reshape x1 -> x0, local copies, waits for them, and re-layouts: 6.27 us -> none  [on_device(): blocks = slots.reshape(slots.shape[0] // PATCH, PATCH, feat_cols)]
  transfers between devices with their start and end apart: 2 -> 0, of which waited for: 2 -> 0; matrix products, arithmetic and copies ran while one was open for 4% -> 0% of each run, Pallas kernels for 0% -> 0%
where the time goes in v1:
time: 118 us
  Pallas kernels  110 us (93%)
  local copies, waits for them, and re-layouts  7.09 us (6%)
    pallas_call x1, Pallas kernels, on_device(): pl.pallas_call(kernel, out_shape=(jax.ShapeDtypeStruct((TOK, NF), BF), ja...  110 us
    unnamed x5, local copies, waits for them, and re-layouts  7.09 us

profile of v1, /device:TPU:1, one launch (start us, length us, event | category | flops | bytes accessed | tf_op | source)
XLA Modules:
  0.0 117.9 jit_solution(4355127653185092914)
XLA Ops:
  0.6 2.2 %copy.6.llm_hbm = bf16[2048,192]{1,0:T(8,128)(2,1)} copy(bf16[2048,192]{0,1:T(8,128)(2,1)} %param.4) | data formatting | bytes 1572864 | tf_op args[0]
  2.8 110.1 %shard_map.59 = (bf16[1024,1536]{1,0:T(8,128)(2,1)}, f32[192,1536]{1,0:T(8,128)}) custom-call(s32[64]{0:T(128)} %slot_ref.1, bf16[2048,192]{1,0:T(8,128)(2,1)} %copy.6.llm_hbm, bf16[1024,1536]{1,0:T(8,128)(2,1)} %pre_hbm.1, bf16[1536,3072]{1,0:T(8,128)(2,1)} %w_hbm.1), custom_call_target="tpu_custom_call" | custom-call | flops 19327352832 | bytes 18874368 | tf_op jit(solution)/shard_map/pallas_call | solution.py:322
  113.0 0.0 copy-start
  113.0 3.9 %copy.9 = bf16[1024,1536]{1,0:T(8,128)(2,1)} copy(bf16[1024,1536]{1,0:T(8,128)(2,1)} %get-tuple-element.8) | data formatting | bytes 6291456
  116.9 0.0 copy-done
  116.9 1.0 copy.10
Async XLA Ops:
  113.0 3.9 %copy-start = (f32[192,1536]{1,0:T(8,128)S(1)}, f32[192,1536]{1,0:T(8,128)}, u32[]{:S(2)}) copy-start(f32[192,1536]{1,0:T(8,128)} %get-tuple-element.5) | copy-start | bytes 3538948

commit v2 on v1

v2 whole, which is shorter than its diff:
```python
import jax
import jax.numpy as jnp
from jax import lax
from jax.experimental import pallas as pl
from jax.experimental.pallas import tpu as pltpu
from jax.sharding import PartitionSpec as P

MESH = pl.DeviceIdType.MESH
BF = jnp.bfloat16
F32 = jnp.float32
NK = 3
TOK = 1024
NF = 1536
GROUPS = ((0, 6), (6, 6), (12, 6), (18, 4), (22, 2))
TO_Y = (3, 1)


def gelu_parts(value):
    inner = 0.7978845608 * (value + 0.044715 * value * value * value)
    tanh_value = jnp.tanh(inner)
    out = 0.5 * value * (1.0 + tanh_value)
    slope = 0.5 * (1.0 + tanh_value) + 0.5 * value * (
        1.0 - tanh_value * tanh_value
    ) * 0.7978845608 * (1.0 + 3.0 * 0.044715 * value * value)
    return (out, slope)


def kernel(
    slot_ref, llm_hbm, pre_hbm, w_hbm, pre, fin,
    llm, w, send_t, recv_t0, recv_t1, recv_t2, send_d, own, sib, hid,
    left, ghacc, send_r, recv_a, recv_r, mine, send_z, recv_z, rhs, slope,
    in_sem, out_sem, t_ss, t_rs, d_ss, d_rs, g_ss, g_rs, s_ss, s_rs, h_ss, h_rs,
    a_ss, a_rs, r_ss, r_rs, z_ss, z_rs,
):
    recv_t = (recv_t0, recv_t1, recv_t2)
    dp = lax.axis_index("dp")
    j = lax.axis_index("tensor")
    y, zlo, c = dp // 4, (dp // 2) % 2, dp % 2
    x, zhi = j // 2, j % 2
    q = dp // 2

    def dev_t(o):
        return (dp, (j + o) % 8)

    def dev_q(o):
        return (((q + o) % 8) * 2 + c, j)

    sibling = (dp - c + (1 - c), j)
    z2 = (dp, 2 * x + (1 - zhi))
    xr, xl, xo = (x + 1) % 4, (x + 3) % 4, (x + 2) % 4
    dev_xr, dev_xl = (dp, 2 * xr + zhi), (dp, 2 * xl + zhi)
    zpart = ((y * 2 + (1 - zlo)) * 2 + c, j)

    def dev_y(o):
        return ((((y + o) % 4) * 2 + zlo) * 2 + c, j)

    def rcopy(src, dst, ss, rs, dev):
        return pltpu.make_async_remote_copy(
            src_ref=src, dst_ref=dst, send_sem=ss, recv_sem=rs, device_id=dev, device_id_type=MESH
        )

    sends = []

    def send(src, dst, ss, rs, dev):
        cp = rcopy(src, dst, ss, rs, dev)
        cp.start()
        sends.append(cp)

    def await_recv(land, ss, rs, dev):
        rcopy(land, land, ss, rs, dev).wait_recv()

    cp_llm = pltpu.make_async_copy(llm_hbm, llm, in_sem.at[0])
    cp_pre = pltpu.make_async_copy(pre_hbm, pre, in_sem.at[1])
    cp_w = pltpu.make_async_copy(w_hbm, w, in_sem.at[2])
    cp_llm.start()
    cp_pre.start()
    cp_w.start()
    barrier = pltpu.get_barrier_semaphore()
    for o in range(1, 8):
        pl.semaphore_signal(barrier, inc=1, device_id=dev_t(o), device_id_type=MESH)
        pl.semaphore_signal(barrier, inc=1, device_id=dev_q(o), device_id_type=MESH)
    pl.semaphore_signal(barrier, inc=1, device_id=sibling, device_id_type=MESH)
    cp_llm.wait()

    @pl.loop(0, 8)
    def _(s):
        for h in range(2):
            lanes = pl.ds(pl.multiple_of(s * 256 + h * 128, 128), 128)
            for cq in range(4):
                for k in range(NK):
                    send_t[k, cq * 2 + h, s] = llm[48 * cq + 16 * k : 48 * cq + 16 * k + 16, lanes]

    pl.semaphore_wait(barrier, 15)

    def place(k, ys, yd, zl):
        off = (ys - yd + 4) % 4
        far = off // 2
        quarter = (1 - far) * (3 - off) + far * (off - 2)
        last = quarter // 3
        return last * (18 + 2 * k) + (1 - last) * (6 * k + 2 * quarter) + zl

    def t_send(k):
        for o in range(1, 8):
            send(
                send_t.at[k, (j + o) % 8], recv_t[k].at[pl.ds(j * 8, 8)],
                t_ss.at[k, o], t_rs.at[k, o], dev_t(o),
            )
        recv_t[k][pl.ds(j * 8, 8)] = send_t[k, j]

    def t_wait_d_send(k):
        for o in range(1, 8):
            await_recv(recv_t[k].at[pl.ds(((j + 8 - o) % 8) * 8, 8)], t_ss.at[k, o], t_rs.at[k, o], dev_t(o))

        @pl.loop(0, 64)
        def _(e):
            send_d[k, e // 8, e % 8] = recv_t[k][slot_ref[e]]

        for o in range(1, 8):
            qd = (q + o) % 8
            send(
                send_d.at[k, qd], own.at[j, place(k, y, qd // 2, zlo)],
                d_ss.at[k, o], d_rs.at[k, o], dev_q(o),
            )
        own[j, 18 + 2 * k + zlo] = send_d[k, q]

    def d_wait(k):
        for o in range(1, 8):
            qs = (q + 8 - o) % 8
            await_recv(
                own.at[j, place(k, qs // 2, y, qs % 2)], d_ss.at[k, o], d_rs.at[k, o], dev_q(o)
            )

    def piece(m, xx, zz):
        first, count = GROUPS[m]
        return own.at[2 * xx + zz, pl.ds(first, count)]

    def half(m, xx, zz, side):
        first, count = GROUPS[m]
        count //= 2
        return own.at[2 * xx + zz, pl.ds(first + side * count, count)]

    def g_send(m, n, ref, dev):
        send(ref, ref, g_ss.at[m, n], g_rs.at[m, n], dev)

    def g_wait(m, n, ref, dev):
        await_recv(ref, g_ss.at[m, n], g_rs.at[m, n], dev)

    oz = 1 - zhi

    def g_a(m):
        g_send(m, 0, piece(m, x, zhi), z2)
        g_send(m, 1, piece(m, x, zhi), dev_xr)
        g_send(m, 2, piece(m, x, zhi), dev_xl)

    def g_b(m):
        g_wait(m, 0, piece(m, x, oz), z2)
        g_send(m, 3, piece(m, x, oz), dev_xr)
        g_send(m, 4, piece(m, x, oz), dev_xl)

    def g_c(m):
        g_wait(m, 1, piece(m, xl, zhi), dev_xl)
        g_send(m, 5, half(m, xl, zhi, 0), dev_xr)
        g_wait(m, 2, piece(m, xr, zhi), dev_xr)
        g_send(m, 6, half(m, xr, zhi, 1), dev_xl)

    def g_e(m):
        g_wait(m, 3, piece(m, xl, oz), dev_xl)
        g_send(m, 7, half(m, xl, oz, 0), dev_xr)
        g_wait(m, 4, piece(m, xr, oz), dev_xr)
        g_send(m, 8, half(m, xr, oz, 1), dev_xl)

    def g_f(m):
        g_wait(m, 5, half(m, xo, zhi, 0), dev_xl)
        g_wait(m, 6, half(m, xo, zhi, 1), dev_xr)
        g_wait(m, 7, half(m, xo, oz, 0), dev_xl)
        g_wait(m, 8, half(m, xo, oz, 1), dev_xr)
        blocks = pl.ds(*GROUPS[m])
        send(
            own.at[:, blocks, pl.ds((1 - c) * 4, 4)], sib.at[:, blocks], s_ss.at[m], s_rs.at[m], sibling
        )

    def sib_wait(m):
        await_recv(sib.at[:, pl.ds(*GROUPS[m])], s_ss.at[m], s_rs.at[m], sibling)

    def hidden_rows(first, count):
        @pl.loop(first, first + count)
        def _(b):
            rows = pl.ds(pl.multiple_of(b * 32, 32), 32)
            value, slope_rows = gelu_parts(pre[rows, :].astype(F32))
            slope[rows, :] = slope_rows
            hid[pl.ds(pl.multiple_of(c * TOK + b * 32, 32), 32), :] = value.astype(BF)

    def down(first, count, store):
        @pl.loop(0, count)
        def _(qq):
            for cq in range(4):
                row = pl.ds(pl.multiple_of(qq * 64 + cq * 16, 16), 16)
                for img in range(8):
                    for h in range(2):
                        left[row, (img * 2 + h) * 128 : (img * 2 + h + 1) * 128] = own[
                            cq * 2 + h, first + qq, img
                        ]

        @pl.loop(0, 6)
        def _(n):
            cols = pl.ds(pl.multiple_of(n * 256, 256), 256)
            prod = jnp.dot(left[0 : count * 64, :], hid[:, cols], preferred_element_type=F32)
            prod = prod.reshape(count, 64, 256)
            for at in range(count):
                store(at, cols, prod[at])

    def down_a(k):
        def store(at, cols, rows):
            send_r[k, at, :, cols] = rows.astype(BF)

        down(6 * k, 2, store)
        for n in range(2):
            send(send_r.at[k, n], recv_a.at[k, n], a_ss.at[k, n], a_rs.at[k, n], dev_y(1 + 2 * n))

    def down_b(k):
        for n in range(2):
            await_recv(recv_a.at[k, n], a_ss.at[k, n], a_rs.at[k, n], dev_y(3 - 2 * n))

        def store(at, cols, rows):
            if at in (1, 2):
                rows += recv_a[k, 2 - at, :, cols].astype(F32)
            send_r[k, 2 + at, :, cols] = rows.astype(BF)

        down(6 * k + 2, 4, store)
        for n in range(2):
            send(
                send_r.at[k, pl.ds(2 + 2 * n, 2)], recv_r.at[k, n],
                r_ss.at[k, n], r_rs.at[k, n], dev_y(TO_Y[n]),
            )

    def down_c(k, chunks):
        def store(at, cols, rows):
            mine[k + at // 2, at % 2, :, cols] = rows

        down(18 + 2 * k, 2 * chunks, store)

    def r_sum(k):
        for n in range(2):
            await_recv(recv_r.at[k, n], r_ss.at[k, n], r_rs.at[k, n], dev_y(TO_Y[1 - n]))

        @pl.loop(0, 4)
        def _(b):
            rows = pl.ds(pl.multiple_of(b * 16, 16), 16)
            for side in range(2):
                zz = zlo if side == 0 else 1 - zlo
                total = mine[k, zz, rows, :]
                for o in range(2):
                    total += recv_r[k, o, zz, rows, :].astype(F32)
                if side == 0:
                    mine[k, zz, rows, :] = total
                else:
                    send_z[k, rows, :] = total.astype(BF)

        send(send_z.at[k], recv_z.at[k], z_ss.at[k], z_rs.at[k], zpart)

    def r_final(k):
        await_recv(recv_z.at[k], z_ss.at[k], z_rs.at[k], zpart)

        @pl.loop(0, 4)
        def _(cq):
            rows = pl.ds(pl.multiple_of(cq * 16, 16), 16)
            total = mine[k, zlo, rows, :] + recv_z[k, rows, :].astype(F32)
            fin[pl.ds(pl.multiple_of(cq * 48 + k * 16, 16), 16), :] = total * (1.0 / 128.0)

    def order_w(b):
        rows = pl.ds(b * 256, 256)
        out = lax.broadcasted_iota(jnp.int32, (384, 384), 1)
        source = ((out >> 6) & 1) * 192 + ((out >> 4) & 3) * 48 + (out >> 7) * 16 + (out & 15)
        perm = (lax.broadcasted_iota(jnp.int32, (384, 384), 0) == source).astype(F32).astype(BF)

        @pl.loop(0, 8)
        def _(u):
            cols = pl.ds(pl.multiple_of(u * 384, 384), 384)
            w[rows, cols] = jnp.dot(w[rows, cols], perm, preferred_element_type=F32).astype(BF)

    def up(g, b):
        def source(at):
            if g < 3:
                return g, 2 * ((y + (2, 3, 1)[at // 2]) % 4) + at % 2
            return at // 2, 2 * y + at % 2

        for at in range(6):
            for cq in range(4):
                for h in range(2):
                    lanes = slice(h * 128, (h + 1) * 128)
                    for p, rows in (
                        (c, own[cq * 2 + h, 6 * g + at, c * 4 + b]),
                        (1 - c, sib[cq * 2 + h, 6 * g + at, b]),
                    ):
                        row = pl.multiple_of(at * 128 + p * 64 + cq * 16, 16)
                        rhs[pl.ds(row, 16), lanes] = rows

        tokens = slice(b * 256, (b + 1) * 256)

        @pl.loop(0, 3)
        def _(n):
            fs = pl.ds(pl.multiple_of(n * 512, 512), 512)
            blocks = []
            for at in range(6):
                k, qq = source(at)
                blocks.append(w[fs, pl.ds(pl.multiple_of(qq * 384 + k * 128, 128), 128)])
            lhs = jnp.concatenate(blocks, axis=1)
            part = jnp.dot(lhs, rhs[...], preferred_element_type=F32)
            if g > 0:
                part += ghacc[fs, tokens]
            if g < 3:
                ghacc[fs, tokens] = part
            else:
                pre[tokens, fs] = (part.T * slope[tokens, fs]).astype(BF)


    t_send(0)
    cp_pre.wait()
    hidden_rows(0, 16)
    t_wait_d_send(0)
    t_send(1)
    t_send(2)
    cp_w.wait()
    order_w(0)
    d_wait(0)
    g_a(0)
    t_wait_d_send(1)
    hidden_rows(16, 4)
    g_b(0)
    t_wait_d_send(2)
    hidden_rows(20, 6)
    g_c(0)
    hidden_rows(26, 6)
    send(hid.at[pl.ds(c * TOK, TOK)], hid.at[pl.ds(c * TOK, TOK)], h_ss.at[0], h_rs.at[0], sibling)
    g_e(0)
    d_wait(1)
    g_a(1)
    order_w(1)
    order_w(2)
    g_b(1)
    g_f(0)
    await_recv(hid.at[pl.ds((1 - c) * TOK, TOK)], h_ss.at[0], h_rs.at[0], sibling)
    down_a(0)
    g_c(1)
    d_wait(2)
    g_a(2)
    order_w(3)
    order_w(4)
    order_w(5)
    g_e(1)
    g_b(2)
    down_b(0)
    sib_wait(0)
    up(0, 0)
    up(0, 1)
    g_f(1)
    down_a(1)
    g_c(2)
    g_a(3)
    up(0, 2)
    up(0, 3)
    sib_wait(1)
    up(1, 0)
    g_e(2)
    g_b(3)
    down_b(1)
    up(1, 1)
    up(1, 2)
    g_f(2)
    down_a(2)
    g_c(3)
    g_a(4)
    g_e(3)
    g_b(4)
    sib_wait(2)
    up(1, 3)
    up(2, 0)
    g_c(4)
    up(2, 1)
    g_f(3)
    g_e(4)
    down_b(2)
    down_c(0, 2)
    r_sum(0)
    r_sum(1)
    g_f(4)
    down_c(2, 1)
    r_sum(2)
    up(2, 2)
    up(2, 3)
    r_final(0)
    sib_wait(3)
    sib_wait(4)
    up(3, 0)
    r_final(1)
    up(3, 1)
    r_final(2)
    up(3, 2)
    up(3, 3)
    for cp in sends:
        cp.wait_send()


def on_device(llm_grad, image_slot, pre_act, w_down):
    dma = pltpu.SemaphoreType.DMA
    any_space = pl.BlockSpec(memory_space=pl.ANY)
    grad_pre, down = pl.pallas_call(
        kernel,
        out_shape=(
            pltpu.VMEM((TOK, NF), BF),
            pltpu.VMEM((192, NF), F32),
        ),
        in_specs=[pl.BlockSpec(memory_space=pltpu.SMEM), any_space, any_space, any_space],
        out_specs=(pl.BlockSpec(memory_space=pltpu.VMEM), pl.BlockSpec(memory_space=pltpu.VMEM)),
        scratch_shapes=[
            pltpu.VMEM((192, 2048), BF),
            pltpu.VMEM((NF, 3072), BF),
            pltpu.VMEM((NK, 8, 8, 16, 128), BF),
            pltpu.VMEM((64, 16, 128), BF),
            pltpu.VMEM((64, 16, 128), BF),
            pltpu.VMEM((64, 16, 128), BF),
            pltpu.VMEM((NK, 8, 8, 16, 128), BF),
            pltpu.VMEM((8, 24, 8, 16, 128), BF),
            pltpu.VMEM((8, 24, 4, 16, 128), BF),
            pltpu.VMEM((2 * TOK, NF), BF),
            pltpu.VMEM((256, 2048), BF),
            pltpu.VMEM((NF, TOK), F32),
            pltpu.VMEM((NK, 6, 64, NF), BF),
            pltpu.VMEM((NK, 2, 64, NF), BF),
            pltpu.VMEM((NK, 2, 2, 64, NF), BF),
            pltpu.VMEM((NK, 2, 64, NF), F32),
            pltpu.VMEM((NK, 64, NF), BF),
            pltpu.VMEM((NK, 64, NF), BF),
            pltpu.VMEM((768, 256), BF),
            pltpu.VMEM((TOK, NF), F32),
            dma((3,)), dma((1,)),
            dma((NK, 8)), dma((NK, 8)), dma((NK, 8)), dma((NK, 8)),
            dma((5, 9)), dma((5, 9)), dma((5,)), dma((5,)), dma((1,)), dma((1,)),
            dma((NK, 2)), dma((NK, 2)), dma((NK, 2)), dma((NK, 2)), dma((NK,)), dma((NK,)),
        ],
        compiler_params=pltpu.CompilerParams(
            collective_id=0, has_side_effects=True, vmem_limit_bytes=56 << 20
        ),
        cost_estimate=pl.CostEstimate(
            flops=19_327_352_832, bytes_accessed=18 << 20, transcendentals=3_000_000
        ),
    )(image_slot, llm_grad.T, pre_act, w_down)
    return (grad_pre, down.T)


def solution(mesh):
    placed = (P("tensor", "dp"), P(), P("dp", "tensor"), P("tensor", None))
    return jax.shard_map(
        on_device,
        mesh=mesh,
        in_specs=placed,
        out_specs=(P("dp", "tensor"), P("tensor", "dp")),
        check_vma=False,
    )
```

time: 118 us -> 112 us (0.949); the launches traced: 118 us -> 110 us
  local copies, waits for them, and re-layouts: 7.09 us -> 2.68 us
  Pallas kernels: 110 us -> 106 us
    unnamed x5 -> x2, local copies, waits for them, and re-layouts: 7.09 us -> 2.68 us
    pallas_call x1, Pallas kernels: 110 us -> 106 us  [on_device(): pl.pallas_call(kernel, out_shape=(pltpu.VMEM((TOK, NF), BF), pltpu.VMEM((...]
where the time goes in v2:
time: 112 us; the launch traced here: 110 us
  Pallas kernels  106 us (95%)
  local copies, waits for them, and re-layouts  2.68 us (2%)
    pallas_call x1, Pallas kernels, on_device(): pl.pallas_call(kernel, out_shape=(pltpu.VMEM((TOK, NF), BF), pltpu.VMEM((...  106 us
    unnamed x2, local copies, waits for them, and re-layouts  2.68 us

profile of v2, /device:TPU:1, one launch (start us, length us, event | category | flops | bytes accessed | tf_op | source)
XLA Modules:
  0.0 109.6 jit_solution(2775101662961987947)
XLA Ops:
  0.6 106.2 %shard_map.59 = (bf16[1024,1536]{1,0:T(8,128)(2,1)S(1)}, f32[192,1536]{1,0:T(8,128)S(1)}) custom-call(s32[64]{0:T(128)} %slot_ref.1, bf16[192,2048]{1,0:T(8,128)(2,1)} %bitcast.3, bf16[1024,1536]{1,0:T(8,128)(2,1)} %pre_hbm.1, bf16[1536,3072]{1,0:T(8,128)(2,1)} %w_hbm.1), custom_call_target="tpu_custom_call" | custom-call | flops 19327352832 | bytes 18874368 | tf_op jit(solution)/shard_map/pallas_call | solution.py:407
  106.9 1.7 %copy.8 = bf16[1024,1536]{1,0:T(8,128)(2,1)} copy(bf16[1024,1536]{1,0:T(8,128)(2,1)S(1)} %get-tuple-element.6) | data formatting | bytes 6291456
  108.5 1.0 copy.9

commit v3 on v2

--- a/solution.py
+++ b/solution.py
@@ -28,7 +28,7 @@
 def kernel(
     slot_ref, llm_hbm, pre_hbm, w_hbm, pre, fin,
     llm, w, send_t, recv_t0, recv_t1, recv_t2, send_d, own, sib, hid,
-    left, ghacc, send_r, recv_a, recv_r, mine, send_z, recv_z, rhs, slope,
+    left, ghacc, send_r, wait_r, recv_a, recv_r, mine, send_z, recv_z, rhs, slope,
     in_sem, out_sem, t_ss, t_rs, d_ss, d_rs, g_ss, g_rs, s_ss, s_rs, h_ss, h_rs,
     a_ss, a_rs, r_ss, r_rs, z_ss, z_rs,
 ):
@@ -201,11 +201,11 @@
                             cq * 2 + h, first + qq, img
                         ]
 
-        @pl.loop(0, 6)
+        @pl.loop(0, 2)
         def _(n):
-            cols = pl.ds(pl.multiple_of(n * 256, 256), 256)
+            cols = pl.ds(pl.multiple_of(n * 768, 768), 768)
             prod = jnp.dot(left[0 : count * 64, :], hid[:, cols], preferred_element_type=F32)
-            prod = prod.reshape(count, 64, 256)
+            prod = prod.reshape(count, 64, 768)
             for at in range(count):
                 store(at, cols, prod[at])
 
@@ -217,21 +217,36 @@
         for n in range(2):
             send(send_r.at[k, n], recv_a.at[k, n], a_ss.at[k, n], a_rs.at[k, n], dev_y(1 + 2 * n))
 
+    def r_send(k, at):
+        n, zz = at // 2, at % 2
+        send(
+            send_r.at[k, 2 + at], recv_r.at[k, n, zz], r_ss.at[k, at], r_rs.at[k, at], dev_y(TO_Y[n])
+        )
+
     def down_b(k):
+        def store(at, cols, rows):
+            if at in (1, 2):
+                wait_r[at - 1, :, cols] = rows
+            else:
+                send_r[k, 2 + at, :, cols] = rows.astype(BF)
+
+        down(6 * k + 2, 4, store)
+        r_send(k, 0)
+        r_send(k, 3)
+
+    def relay(k):
         for n in range(2):
             await_recv(recv_a.at[k, n], a_ss.at[k, n], a_rs.at[k, n], dev_y(3 - 2 * n))
 
-        def store(at, cols, rows):
-            if at in (1, 2):
-                rows += recv_a[k, 2 - at, :, cols].astype(F32)
-            send_r[k, 2 + at, :, cols] = rows.astype(BF)
-
-        down(6 * k + 2, 4, store)
-        for n in range(2):
-            send(
-                send_r.at[k, pl.ds(2 + 2 * n, 2)], recv_r.at[k, n],
-                r_ss.at[k, n], r_rs.at[k, n], dev_y(TO_Y[n]),
-            )
+        @pl.loop(0, 4)
+        def _(b):
+            rows = pl.ds(pl.multiple_of(b * 16, 16), 16)
+            for n in range(2):
+                total = wait_r[n, rows, :] + recv_a[k, 1 - n, rows, :].astype(F32)
+                send_r[k, 3 + n, rows, :] = total.astype(BF)
+
+        r_send(k, 1)
+        r_send(k, 2)
 
     def down_c(k, chunks):
         def store(at, cols, rows):
@@ -240,8 +255,9 @@
         down(18 + 2 * k, 2 * chunks, store)
 
     def r_sum(k):
-        for n in range(2):
-            await_recv(recv_r.at[k, n], r_ss.at[k, n], r_rs.at[k, n], dev_y(TO_Y[1 - n]))
+        for at in range(4):
+            n, zz = at // 2, at % 2
+            await_recv(recv_r.at[k, n, zz], r_ss.at[k, at], r_rs.at[k, at], dev_y(TO_Y[1 - n]))
 
         @pl.loop(0, 4)
         def _(b):
@@ -268,7 +284,7 @@
             fin[pl.ds(pl.multiple_of(cq * 48 + k * 16, 16), 16), :] = total * (1.0 / 128.0)
 
     def order_w(b):
-        rows = pl.ds(b * 256, 256)
+        rows = pl.ds(b * 512, 512)
         out = lax.broadcasted_iota(jnp.int32, (384, 384), 1)
         source = ((out >> 6) & 1) * 192 + ((out >> 4) & 3) * 48 + (out >> 7) * 16 + (out & 15)
         perm = (lax.broadcasted_iota(jnp.int32, (384, 384), 0) == source).astype(F32).astype(BF)
@@ -279,36 +295,39 @@
             w[rows, cols] = jnp.dot(w[rows, cols], perm, preferred_element_type=F32).astype(BF)
 
     def up(g, b):
+        first, count = GROUPS[g]
+
         def source(at):
             if g < 3:
                 return g, 2 * ((y + (2, 3, 1)[at // 2]) % 4) + at % 2
-            return at // 2, 2 * y + at % 2
-
-        for at in range(6):
+            return 2 * (g - 3) + at // 2, 2 * y + at % 2
+
+        for at in range(count):
             for cq in range(4):
-                for h in range(2):
-                    lanes = slice(h * 128, (h + 1) * 128)
+                for n in range(4):
+                    lanes = slice(n * 128, (n + 1) * 128)
+                    img, h = 2 * b + n // 2, n % 2
                     for p, rows in (
-                        (c, own[cq * 2 + h, 6 * g + at, c * 4 + b]),
-                        (1 - c, sib[cq * 2 + h, 6 * g + at, b]),
+                        (c, own[cq * 2 + h, first + at, c * 4 + img]),
+                        (1 - c, sib[cq * 2 + h, first + at, img]),
                     ):
                         row = pl.multiple_of(at * 128 + p * 64 + cq * 16, 16)
                         rhs[pl.ds(row, 16), lanes] = rows
 
-        tokens = slice(b * 256, (b + 1) * 256)
-
-        @pl.loop(0, 3)
+        tokens = slice(b * 512, (b + 1) * 512)
+
+        @pl.loop(0, 2)
         def _(n):
-            fs = pl.ds(pl.multiple_of(n * 512, 512), 512)
+            fs = pl.ds(pl.multiple_of(n * 768, 768), 768)
             blocks = []
-            for at in range(6):
+            for at in range(count):
                 k, qq = source(at)
                 blocks.append(w[fs, pl.ds(pl.multiple_of(qq * 384 + k * 128, 128), 128)])
             lhs = jnp.concatenate(blocks, axis=1)
-            part = jnp.dot(lhs, rhs[...], preferred_element_type=F32)
+            part = jnp.dot(lhs, rhs[0 : count * 128, :], preferred_element_type=F32)
             if g > 0:
                 part += ghacc[fs, tokens]
-            if g < 3:
+            if g < 4:
                 ghacc[fs, tokens] = part
             else:
                 pre[tokens, fs] = (part.T * slope[tokens, fs]).astype(BF)
@@ -336,7 +355,6 @@
     d_wait(1)
     g_a(1)
     order_w(1)
-    order_w(2)
     g_b(1)
     g_f(0)
     await_recv(hid.at[pl.ds((1 - c) * TOK, TOK)], h_ss.at[0], h_rs.at[0], sibling)
@@ -344,59 +362,54 @@
     g_c(1)
     d_wait(2)
     g_a(2)
-    order_w(3)
-    order_w(4)
-    order_w(5)
+    down_b(0)
+    order_w(2)
     g_e(1)
     g_b(2)
-    down_b(0)
+    relay(0)
     sib_wait(0)
     up(0, 0)
-    up(0, 1)
     g_f(1)
     down_a(1)
     g_c(2)
     g_a(3)
-    up(0, 2)
-    up(0, 3)
+    down_b(1)
+    up(0, 1)
+    g_e(2)
+    g_b(3)
+    relay(1)
     sib_wait(1)
     up(1, 0)
-    g_e(2)
-    g_b(3)
-    down_b(1)
     up(1, 1)
-    up(1, 2)
     g_f(2)
     down_a(2)
     g_c(3)
     g_a(4)
+    down_b(2)
     g_e(3)
     g_b(4)
+    g_c(4)
+    relay(2)
     sib_wait(2)
-    up(1, 3)
     up(2, 0)
-    g_c(4)
-    up(2, 1)
     g_f(3)
     g_e(4)
-    down_b(2)
     down_c(0, 2)
     r_sum(0)
     r_sum(1)
+    sib_wait(3)
+    up(2, 1)
+    up(3, 0)
     g_f(4)
     down_c(2, 1)
     r_sum(2)
-    up(2, 2)
-    up(2, 3)
+    up(3, 1)
     r_final(0)
-    sib_wait(3)
+    r_final(1)
     sib_wait(4)
-    up(3, 0)
-    r_final(1)
-    up(3, 1)
+    up(4, 0)
     r_final(2)
-    up(3, 2)
-    up(3, 3)
+    up(4, 1)
     for cp in sends:
         cp.wait_send()
 
@@ -426,17 +439,18 @@
             pltpu.VMEM((256, 2048), BF),
             pltpu.VMEM((NF, TOK), F32),
             pltpu.VMEM((NK, 6, 64, NF), BF),
+            pltpu.VMEM((2, 64, NF), F32),
             pltpu.VMEM((NK, 2, 64, NF), BF),
             pltpu.VMEM((NK, 2, 2, 64, NF), BF),
             pltpu.VMEM((NK, 2, 64, NF), F32),
             pltpu.VMEM((NK, 64, NF), BF),
             pltpu.VMEM((NK, 64, NF), BF),
-            pltpu.VMEM((768, 256), BF),
+            pltpu.VMEM((768, 512), BF),
             pltpu.VMEM((TOK, NF), F32),
             dma((3,)), dma((1,)),
             dma((NK, 8)), dma((NK, 8)), dma((NK, 8)), dma((NK, 8)),
             dma((5, 9)), dma((5, 9)), dma((5,)), dma((5,)), dma((1,)), dma((1,)),
-            dma((NK, 2)), dma((NK, 2)), dma((NK, 2)), dma((NK, 2)), dma((NK,)), dma((NK,)),
+            dma((NK, 2)), dma((NK, 2)), dma((NK, 4)), dma((NK, 4)), dma((NK,)), dma((NK,)),
         ],
         compiler_params=pltpu.CompilerParams(
             collective_id=0, has_side_effects=True, vmem_limit_bytes=56 << 20

time: 112 us -> 105 us (0.938); the launches traced: 110 us -> 105 us
  Pallas kernels: 106 us -> 102 us
    pallas_call x1, Pallas kernels: 106 us -> 102 us  [on_device(): pl.pallas_call(kernel, out_shape=(pltpu.VMEM((TOK, NF), BF), pltpu.VMEM((...]
where the time goes in v3:
time: 105 us
  Pallas kernels  102 us (97%)
  local copies, waits for them, and re-layouts  2.68 us (3%)
    pallas_call x1, Pallas kernels, on_device(): pl.pallas_call(kernel, out_shape=(pltpu.VMEM((TOK, NF), BF), pltpu.VMEM((...  102 us
    unnamed x2, local copies, waits for them, and re-layouts  2.68 us

profile of v3, /device:TPU:1, one launch (start us, length us, event | category | flops | bytes accessed | tf_op | source)
XLA Modules:
  0.0 105.0 jit_solution(9542006187020047594)
XLA Ops:
  0.6 101.6 %shard_map.59 = (bf16[1024,1536]{1,0:T(8,128)(2,1)S(1)}, f32[192,1536]{1,0:T(8,128)S(1)}) custom-call(s32[64]{0:T(128)} %slot_ref.1, bf16[192,2048]{1,0:T(8,128)(2,1)} %bitcast.3, bf16[1024,1536]{1,0:T(8,128)(2,1)} %pre_hbm.1, bf16[1536,3072]{1,0:T(8,128)(2,1)} %w_hbm.1), custom_call_target="tpu_custom_call" | custom-call | flops 19327352832 | bytes 18874368 | tf_op jit(solution)/shard_map/pallas_call | solution.py:420
  102.3 1.7 %copy.8 = bf16[1024,1536]{1,0:T(8,128)(2,1)} copy(bf16[1024,1536]{1,0:T(8,128)(2,1)S(1)} %get-tuple-element.6) | data formatting | bytes 6291456
  103.9 1.0 copy.9

commit v4 on v3

--- a/solution.py
+++ b/solution.py
@@ -400,16 +400,16 @@
     sib_wait(3)
     up(2, 1)
     up(3, 0)
+    up(3, 1)
     g_f(4)
     down_c(2, 1)
     r_sum(2)
-    up(3, 1)
     r_final(0)
     r_final(1)
     sib_wait(4)
     up(4, 0)
+    up(4, 1)
     r_final(2)
-    up(4, 1)
     for cp in sends:
         cp.wait_send()
 

time: 105 us -> 104 us (level)
  Pallas kernels: 102 us -> 100 us
    pallas_call x1, Pallas kernels: 102 us -> 100 us  [on_device(): pl.pallas_call(kernel, out_shape=(pltpu.VMEM((TOK, NF), BF), pltpu.VMEM((...]
where the time goes in v4:
time: 104 us; the launch traced here: 103 us
  Pallas kernels  100 us (96%)
  local copies, waits for them, and re-layouts  2.68 us (3%)
    pallas_call x1, Pallas kernels, on_device(): pl.pallas_call(kernel, out_shape=(pltpu.VMEM((TOK, NF), BF), pltpu.VMEM((...  100 us
    unnamed x2, local copies, waits for them, and re-layouts  2.68 us

profile of v4, /device:TPU:1, one launch (start us, length us, event | category | flops | bytes accessed | tf_op | source)
XLA Modules:
  0.0 103.4 jit_solution(5861063275053453027)
XLA Ops:
  0.6 100.0 %shard_map.59 = (bf16[1024,1536]{1,0:T(8,128)(2,1)S(1)}, f32[192,1536]{1,0:T(8,128)S(1)}) custom-call(s32[64]{0:T(128)} %slot_ref.1, bf16[192,2048]{1,0:T(8,128)(2,1)} %bitcast.3, bf16[1024,1536]{1,0:T(8,128)(2,1)} %pre_hbm.1, bf16[1536,3072]{1,0:T(8,128)(2,1)} %w_hbm.1), custom_call_target="tpu_custom_call" | custom-call | flops 19327352832 | bytes 18874368 | tf_op jit(solution)/shard_map/pallas_call | solution.py:420
  100.7 1.7 %copy.8 = bf16[1024,1536]{1,0:T(8,128)(2,1)} copy(bf16[1024,1536]{1,0:T(8,128)(2,1)S(1)} %get-tuple-element.6) | data formatting | bytes 6291456
  102.3 1.0 copy.9

commit v5 on v4

--- a/solution.py
+++ b/solution.py
@@ -401,11 +401,11 @@
     up(2, 1)
     up(3, 0)
     up(3, 1)
+    r_final(0)
     g_f(4)
     down_c(2, 1)
+    r_final(1)
     r_sum(2)
-    r_final(0)
-    r_final(1)
     sib_wait(4)
     up(4, 0)
     up(4, 1)

time: 104 us -> 105 us (level); the launches traced: 103 us -> 103 us
  no operation moved by 1% of the time
where the time goes in v5:
time: 105 us; the launch traced here: 103 us
  Pallas kernels  99.9 us (95%)
  local copies, waits for them, and re-layouts  2.68 us (3%)
    pallas_call x1, Pallas kernels, on_device(): pl.pallas_call(kernel, out_shape=(pltpu.VMEM((TOK, NF), BF), pltpu.VMEM((...  99.9 us
    unnamed x2, local copies, waits for them, and re-layouts  2.68 us

profile of v5, /device:TPU:1, one launch (start us, length us, event | category | flops | bytes accessed | tf_op | source)
XLA Modules:
  0.0 103.2 jit_solution(12066831969892643245)
XLA Ops:
  0.6 99.9 %shard_map.59 = (bf16[1024,1536]{1,0:T(8,128)(2,1)S(1)}, f32[192,1536]{1,0:T(8,128)S(1)}) custom-call(s32[64]{0:T(128)} %slot_ref.1, bf16[192,2048]{1,0:T(8,128)(2,1)} %bitcast.3, bf16[1024,1536]{1,0:T(8,128)(2,1)} %pre_hbm.1, bf16[1536,3072]{1,0:T(8,128)(2,1)} %w_hbm.1), custom_call_target="tpu_custom_call" | custom-call | flops 19327352832 | bytes 18874368 | tf_op jit(solution)/shard_map/pallas_call | solution.py:420
  100.5 1.7 %copy.8 = bf16[1024,1536]{1,0:T(8,128)(2,1)} copy(bf16[1024,1536]{1,0:T(8,128)(2,1)S(1)} %get-tuple-element.6) | data formatting | bytes 6291456
  102.2 1.0 copy.9
